TPU v7x, 512 devices: a whole 4x4x16 slice. The times are simulated.
512 devices in a mesh: sec: 32 (over z_lo, x, core), ch: 16 (over z_hi, y).
Axes of the slice: x: 4, y: 4, z: 16 (z_hi: 4, z_lo: 4; z = z_hi * 4 + z_lo), core: 2. Of those that a mesh axis runs over, the one named last changes fastest.
Arguments:
- diag_blocks: float32 [32, 512, 512], P('sec', None, 'ch'), as said below
- lower_blocks: float32 [32, 512, 512], P('sec', None, 'ch'), as said below
- upper_blocks: float32 [32, 512, 512], P('sec', None, 'ch'), as said below
- sources: float32 [32, 512, 4096], P('sec', None, 'ch'), may hold values from -6 to 6
Outputs:
- reduced_diag: float32 [32, 512, 512], P('sec', None, 'ch')
- reduced_sources: float32 [32, 512, 4096], P('sec', None, 'ch')
Inputs may be any that keep to these rules, and one draw needn't show every extreme that they name: `diag_blocks`: every block's diagonal entries lie between 4 and 8; every off-diagonal entry has magnitude at most 2.1 / sqrt(512). `lower_blocks`: every entry has magnitude below 3.7. `upper_blocks`: every entry has magnitude below 3.7.
All inputs are finite; a program needn't handle non-finite values.
Results may differ from a plain program's by a relative error of at most 0.0001.
Values sent between devices are 32-bit elements; how exact they have to be, the bound alone decides.
A program may use at most 64 MiB of HBM per device.

v0:
```python
import jax
import jax.numpy as jnp
from jax import lax
from jax.sharding import PartitionSpec as P

LEVELS = 3


def shifted(x, axis, by):
    size = lax.axis_size(axis)
    pairs = [(i, i + by) for i in range(size) if 0 <= i + by < size]
    return lax.ppermute(x, axis, pairs)


def product(left, right):
    return jnp.dot(left, right, precision=lax.Precision.HIGHEST, preferred_element_type=jnp.float32)


def first_inverse(center):
    diag_vals = jnp.diagonal(center)
    recip = 1.0 / diag_vals
    eye_mat = jnp.eye(center.shape[-1], dtype=jnp.float32)
    off_part = center - diag_vals[:, None] * eye_mat
    return recip[:, None] * eye_mat - recip[:, None] * off_part * recip[None, :]


def shards(diag_blocks, lower_blocks, upper_blocks, sources):
    center = diag_blocks[0]
    down_link = lower_blocks[0]
    up_link = upper_blocks[0]
    source = sources[0]
    col_count = center.shape[1]
    offset = lax.axis_index("ch") * col_count
    for level_no in range(LEVELS):
        stride = 2**level_no
        is_last = level_no == LEVELS - 1
        whole_center, whole_down, whole_up = (
            lax.all_gather(center, "ch", axis=1, tiled=True),
            lax.all_gather(down_link, "ch", axis=1, tiled=True),
            lax.all_gather(up_link, "ch", axis=1, tiled=True),
        )
        seed_inv = first_inverse(whole_center)
        seed_cols = lax.dynamic_slice_in_dim(seed_inv, offset, col_count, 1)
        inverse_cols = 2.0 * seed_cols - product(seed_inv, product(whole_center, seed_cols))
        inverse = lax.all_gather(inverse_cols, "ch", axis=1, tiled=True)
        down_sol = product(inverse, down_link)
        up_sol = product(inverse, up_link)
        source_sol = product(inverse, source)
        if is_last:
            down_pair = up_sol[None]
            up_pair = down_sol[None]
        else:
            down_pair = jnp.stack([up_sol, down_sol])
            up_pair = jnp.stack([down_sol, up_sol])
        below_pair, below_source = shifted((down_pair, source_sol), "sec", stride)
        above_pair, above_source = shifted((up_pair, source_sol), "sec", -stride)
        new_center = center - product(whole_down, below_pair[0]) - product(whole_up, above_pair[0])
        source = source - product(whole_down, below_source) - product(whole_up, above_source)
        if not is_last:
            down_link = -product(whole_down, below_pair[1])
            up_link = -product(whole_up, above_pair[1])
        center = new_center
    return (center[None], source[None])


def solution(mesh):
    placed = (
        P("sec", None, "ch"),
        P("sec", None, "ch"),
        P("sec", None, "ch"),
        P("sec", None, "ch"),
    )
    return jax.shard_map(
        shards,
        mesh=mesh,
        in_specs=placed,
        out_specs=(P("sec", None, "ch"), P("sec", None, "ch")),
        check_vma=False,
    )
```

profile of v0, /device:TPU:6, one launch (start us, length us, event | category | flops | bytes accessed | tf_op | source)
XLA Modules:
  0.0 962.0 jit_solution(8823493597186743005)
XLA Ops:
  7.2 0.7 all-gather.34.cloned.1.call-update
  8.0 84.9 %all-gather.34.cloned.1.call-done = f32[1,512,512]{1,2,0:T(8,128)} async-done(((f32[1,512,32]{1,2,0:T(8,128)}), f32[1,512,512]{1,2,0:T(8,128)}) %all-gather.34.cloned.1.call-update) | async-done | bytes 1048592 | tf_op jit(solution)/shard_map/all_gather | solution.py:38
  92.9 8.8 gather_fusion
  101.9 0.7 fusion.28
  102.6 1.4 convolution_subtract_fusion.4
  105.4 70.8 %all-gather.16.cloned.1.call-done = f32[512,512]{0,1:T(8,128)} async-done(((f32[512,32]{0,1:T(8,128)}), f32[512,512]{0,1:T(8,128)}) %all-gather.16.cloned.1.call-update) | async-done | bytes 1048592 | tf_op jit(solution)/shard_map/all_gather | solution.py:45
  176.2 2.0 convolution_bitcast_fusion.8
  178.3 0.7 convolution_bitcast_fusion.9
  179.0 2.2 collective-permute-start.1
  181.3 2.2 collective-permute-start
  183.5 67.7 %all-gather.38.cloned.1.call-done = f32[1,512,512]{1,2,0:T(8,128)} async-done(((f32[1,512,32]{1,2,0:T(8,128)}), f32[1,512,512]{1,2,0:T(8,128)}) %all-gather.38.cloned.1.call-update) | async-done | bytes 1048592 | tf_op jit(solution)/shard_map/all_gather | solution.py:40
  251.3 1.9 convolution_bitcast_fusion.6
  253.2 73.0 %all-gather.36.cloned.1.call-done = f32[1,512,512]{1,2,0:T(8,128)} async-done(((f32[1,512,32]{1,2,0:T(8,128)}), f32[1,512,512]{1,2,0:T(8,128)}) %all-gather.36.cloned.1.call-update) | async-done | bytes 1048592 | tf_op jit(solution)/shard_map/all_gather | solution.py:39
  326.2 2.6 fusion.9
  328.8 72.8 %all-gather.20.cloned.1.call-done = f32[512,512]{0,1:T(8,128)} async-done(((f32[512,32]{0,1:T(8,128)}), f32[512,512]{0,1:T(8,128)}) %all-gather.20.cloned.1.call-update) | async-done | bytes 1048592 | tf_op jit(solution)/shard_map/all_gather | solution.py:38
  401.7 8.7 gather_fusion.1
  410.6 1.8 fusion.26
  412.4 1.4 convolution_subtract_fusion.6
  414.0 1.3 convolution_negate_fusion.2
  415.4 1.3 convolution_negate_fusion.3
  416.8 69.3 %all-gather.22.cloned.1.call-done = f32[512,512]{0,1:T(8,128)} async-done(((f32[512,32]{0,1:T(8,128)}), f32[512,512]{0,1:T(8,128)}) %all-gather.22.cloned.1.call-update) | async-done | bytes 1048592 | tf_op jit(solution)/shard_map/all_gather | solution.py:45
  486.1 2.0 convolution_bitcast_fusion.5
  488.1 0.7 convolution_bitcast_fusion.4
  488.9 2.8 collective-permute-start.3
  491.7 5.5 collective-permute-start.2
  497.2 64.5 %all-gather.24.cloned.1.call-done = f32[512,512]{0,1:T(8,128)} async-done(((f32[512,32]{0,1:T(8,128)}), f32[512,512]{0,1:T(8,128)}) %all-gather.24.cloned.1.call-update) | async-done | bytes 1048592 | tf_op jit(solution)/shard_map/all_gather | solution.py:40
  561.7 1.9 fusion.18
  563.7 73.1 %all-gather.18.cloned.1.call-done = f32[512,512]{0,1:T(8,128)} async-done(((f32[512,32]{0,1:T(8,128)}), f32[512,512]{0,1:T(8,128)}) %all-gather.18.cloned.1.call-update) | async-done | bytes 1048592 | tf_op jit(solution)/shard_map/all_gather | solution.py:39
  636.8 2.6 fusion.7
  639.4 72.4 %all-gather.28.cloned.1.call-done = f32[512,512]{0,1:T(8,128)} async-done(((f32[512,32]{0,1:T(8,128)}), f32[512,512]{0,1:T(8,128)}) %all-gather.28.cloned.1.call-update) | async-done | bytes 1048592 | tf_op jit(solution)/shard_map/all_gather | solution.py:38
  711.8 8.5 gather_fusion.2
  720.6 1.8 fusion.24
  722.4 1.4 convolution_subtract_fusion.5
  723.9 1.4 convolution_negate_fusion
  725.4 3.7 fusion.16
  729.1 2.4 collective-permute-start.7
  731.5 2.1 collective-permute-start.6
  733.8 4.7 collective-permute-done.7
  738.5 2.1 convolution_bitcast_fusion
  740.6 1.7 collective-permute-done.6
  742.3 2.1 fusion.4
  744.4 1.4 convolution_negate_fusion.1
  745.9 1.9 fusion.34
  747.7 2.5 collective-permute-start.9
  750.2 8.1 collective-permute-start.8
  758.3 10.5 %collective-permute-done.9 = f32[512,256]{1,0:T(8,128)S(1)} collective-permute-done((f32[512,256]{1,0:T(8,128)S(1)}, f32[512,256]{1,0:T(8,128)S(1)}, u32[]{:S(2)}, u32[]{:S(2)}) %collective-permute-start.9) | collective-permute-done | bytes 524320 | tf_op jit(solution)/shard_map/ppermute | solution.py:12
  768.9 1.1 fusion.35
  770.0 4.2 collective-permute-done.8
  774.2 1.2 fusion
  775.4 20.2 %all-gather.30.cloned.1.call-done = f32[512,512]{0,1:T(8,128)} async-done(((f32[512,32]{0,1:T(8,128)}), f32[512,512]{0,1:T(8,128)}) %all-gather.30.cloned.1.call-update) | async-done | bytes 1048592 | tf_op jit(solution)/shard_map/all_gather | solution.py:45
  795.6 3.1 fusion.36
  798.7 3.9 collective-permute-start.11
  802.6 4.5 collective-permute-start.10
  807.1 0.7 convolution_bitcast_fusion.2
  807.9 3.7 collective-permute-start.5
  811.6 0.7 convolution_bitcast_fusion.3
  812.3 4.7 collective-permute-start.4
  817.0 54.6 %all-gather.32.cloned.1.call-done = f32[512,512]{0,1:T(8,128)} async-done(((f32[512,32]{0,1:T(8,128)}), f32[512,512]{0,1:T(8,128)}) %all-gather.32.cloned.1.call-update) | async-done | bytes 1048592 | tf_op jit(solution)/shard_map/all_gather | solution.py:40
  871.6 2.0 fusion.19
  873.7 73.4 %all-gather.26.cloned.1.call-done = f32[512,512]{0,1:T(8,128)} async-done(((f32[512,32]{0,1:T(8,128)}), f32[512,512]{0,1:T(8,128)}) %all-gather.26.cloned.1.call-update) | async-done | bytes 1048592 | tf_op jit(solution)/shard_map/all_gather | solution.py:39
  947.1 2.6 fusion.6
  949.7 2.2 fusion.37
  952.0 2.1 fusion.2
  954.1 1.0 copy.17
  (91 shorter events, 2.8 us)
Async XLA Ops:
  7.2 85.7 %all-gather.34.cloned.1.call-start = ((), (), s32[]{:S(2)}) async-start(), calls=%async_computation.9 | async-start | bytes 1114112 | tf_op jit(solution)/shard_map/all_gather | solution.py:38
  7.9 168.3 %all-gather.16.cloned.1.call-start = ((), (), s32[]{:S(2)}) async-start(), calls=%async_computation | async-start | bytes 1114112 | tf_op jit(solution)/shard_map/all_gather | solution.py:45
  92.9 8.8 copy-start.2
  104.0 72.2 %copy-start.23 = (f32[1,512,32]{1,2,0:T(8,128)S(1)}, f32[1,512,32]{1,2,0:T(8,128)}, u32[]{:S(2)}) copy-start(f32[1,512,32]{1,2,0:T(8,128)} %param.5) | copy-start | bytes 196612
  104.0 147.2 %all-gather.38.cloned.1.call-start = ((), (), s32[]{:S(2)}) async-start(), calls=%async_computation.11 | async-start | bytes 1114112 | tf_op jit(solution)/shard_map/all_gather | solution.py:40
  104.8 221.4 %all-gather.36.cloned.1.call-start = ((), (), s32[]{:S(2)}) async-start(), calls=%async_computation.10 | async-start | bytes 1114112 | tf_op jit(solution)/shard_map/all_gather | solution.py:39
  105.3 72.9 %copy-start.22 = (f32[1,512,32]{1,2,0:T(8,128)S(1)}, f32[1,512,32]{1,2,0:T(8,128)}, u32[]{:S(2)}) copy-start(f32[1,512,32]{1,2,0:T(8,128)} %param.6) | copy-start | bytes 196612
  105.4 296.3 %all-gather.20.cloned.1.call-start = ((), (), s32[]{:S(2)}) async-start(), calls=%async_computation.2 | async-start | bytes 1114112 | tf_op jit(solution)/shard_map/all_gather | solution.py:38
  176.2 2.1 copy-start.5
  179.0 72.2 %collective-permute-start.1 = (f32[2,512,32]{1,2,0:T(8,128)S(1)}, f32[2,512,32]{1,2,0:T(8,128)S(1)}, u32[]{:S(2)}, u32[]{:S(2)}) collective-permute-start(f32[2,512,32]{1,2,0:T(8,128)S(1)} %get-tuple-element.9), channel_id=1, source_target_pairs={{16,0},{32,16},{48,32},{64,48},{80,64},{96,80},{112,96},{128,112},... | collective-permute-start | bytes 393224 | tf_op jit(solution)/shard_map/ppermute | solution.py:12
  181.3 144.9 %copy-start.24 = (f32[1,512,32]{1,2,0:T(8,128)S(1)}, f32[1,512,32]{1,2,0:T(8,128)}, u32[]{:S(2)}) copy-start(f32[1,512,32]{1,2,0:T(8,128)} %param.4) | copy-start | bytes 196612
  181.3 144.9 %collective-permute-start = (f32[2,512,32]{1,2,0:T(8,128)S(1)}, f32[2,512,32]{1,2,0:T(8,128)S(1)}, u32[]{:S(2)}, u32[]{:S(2)}) collective-permute-start(f32[2,512,32]{1,2,0:T(8,128)S(1)} %get-tuple-element.8), channel_id=1, source_target_pairs={{0,16},{16,32},{32,48},{48,64},{64,80},{80,96},{96,112},{112,128},... | collective-permute-start | bytes 393224 | tf_op jit(solution)/shard_map/ppermute | solution.py:12
  328.8 157.3 %all-gather.22.cloned.1.call-start = ((), (), s32[]{:S(2)}) async-start(), calls=%async_computation.3 | async-start | bytes 1114112 | tf_op jit(solution)/shard_map/all_gather | solution.py:45
  401.7 8.7 copy-start.1
  410.6 3.4 copy-start.11
  412.4 3.0 copy-start.3
  413.9 147.8 %all-gather.24.cloned.1.call-start = ((), (), s32[]{:S(2)}) async-start(), calls=%async_computation.4 | async-start | bytes 1114112 | tf_op jit(solution)/shard_map/all_gather | solution.py:40
  415.3 221.4 %all-gather.18.cloned.1.call-start = ((), (), s32[]{:S(2)}) async-start(), calls=%async_computation.1 | async-start | bytes 1114112 | tf_op jit(solution)/shard_map/all_gather | solution.py:39
  416.7 69.4 %copy-start.20 = (f32[32,512]{1,0:T(8,128)S(1)}, f32[32,512]{1,0:T(8,128)}, u32[]{:S(2)}) copy-start(f32[32,512]{1,0:T(8,128)} %convolution_negate_fusion.2) | copy-start | bytes 196612
  416.7 71.4 %copy-start.21 = (f32[32,512]{1,0:T(8,128)S(1)}, f32[32,512]{1,0:T(8,128)}, u32[]{:S(2)}) copy-start(f32[32,512]{1,0:T(8,128)} %convolution_negate_fusion.3) | copy-start | bytes 196612
  416.7 295.1 %all-gather.28.cloned.1.call-start = ((), (), s32[]{:S(2)}) async-start(), calls=%async_computation.6 | async-start | bytes 1114112 | tf_op jit(solution)/shard_map/all_gather | solution.py:38
  486.1 2.1 copy-start.8
  488.9 72.8 %collective-permute-start.3 = (f32[2,512,32]{1,2,0:T(8,128)S(1)}, f32[2,512,32]{1,2,0:T(8,128)S(1)}, u32[]{:S(2)}, u32[]{:S(2)}) collective-permute-start(f32[2,512,32]{1,2,0:T(8,128)S(1)} %get-tuple-element.7), channel_id=1, source_target_pairs={{32,0},{48,16},{64,32},{80,48},{96,64},{112,80},{128,96},{144,112}... | collective-permute-start | bytes 393224 | tf_op jit(solution)/shard_map/ppermute | solution.py:12
  491.7 145.1 %copy-start.17 = (f32[512,32]{0,1:T(8,128)S(1)}, f32[512,32]{0,1:T(8,128)}, u32[]{:S(2)}) copy-start(f32[512,32]{0,1:T(8,128)} %fusion.9) | copy-start | bytes 196612
  491.7 145.1 %collective-permute-start.2 = (f32[2,512,32]{1,2,0:T(8,128)S(1)}, f32[2,512,32]{1,2,0:T(8,128)S(1)}, u32[]{:S(2)}, u32[]{:S(2)}) collective-permute-start(f32[2,512,32]{1,2,0:T(8,128)S(1)} %get-tuple-element.6), channel_id=1, source_target_pairs={{0,32},{16,48},{32,64},{48,80},{64,96},{80,112},{96,128},{112,144}... | collective-permute-start | bytes 393224 | tf_op jit(solution)/shard_map/ppermute | solution.py:12
  639.4 156.2 %all-gather.30.cloned.1.call-start = ((), (), s32[]{:S(2)}) async-start(), calls=%async_computation.7 | async-start | bytes 1114112 | tf_op jit(solution)/shard_map/all_gather | solution.py:45
  711.8 8.5 copy-start
  722.4 1.5 copy-start.6
  723.9 147.8 %all-gather.32.cloned.1.call-start = ((), (), s32[]{:S(2)}) async-start(), calls=%async_computation.8 | async-start | bytes 1114112 | tf_op jit(solution)/shard_map/all_gather | solution.py:40
  725.3 8.3 copy-start.15
  725.3 221.8 %all-gather.26.cloned.1.call-start = ((), (), s32[]{:S(2)}) async-start(), calls=%async_computation.5 | async-start | bytes 1114112 | tf_op jit(solution)/shard_map/all_gather | solution.py:39
  729.1 9.4 copy-start.12
  729.1 9.4 collective-permute-start.7
  731.5 10.8 %collective-permute-start.6 = (f32[512,256]{1,0:T(8,128)}, f32[512,256]{1,0:T(8,128)}, u32[]{:S(2)}, u32[]{:S(2)}) collective-permute-start(f32[512,256]{1,0:T(8,128)} %fusion.16), channel_id=1, source_target_pairs={{0,16},{16,32},{32,48},{48,64},{64,80},{80,96},{96,112},{112,128},... | collective-permute-start | bytes 1572872 | tf_op jit(solution)/shard_map/ppermute | solution.py:12
  740.6 3.8 copy-start.4
  744.4 1.4 copy-start.9
  745.8 23.0 %copy-start.7 = (f32[512,512]{0,1:T(8,128)S(1)}, f32[512,512]{0,1:T(8,128)}, u32[]{:S(2)}) copy-start(f32[512,512]{0,1:T(8,128)} %all-gather.24.cloned.1.call-done) | copy-start | bytes 3145732
  747.7 21.1 %collective-permute-start.9 = (f32[512,256]{1,0:T(8,128)S(1)}, f32[512,256]{1,0:T(8,128)S(1)}, u32[]{:S(2)}, u32[]{:S(2)}) collective-permute-start(f32[512,256]{1,0:T(8,128)S(1)} %fusion.34), channel_id=1, source_target_pairs={{32,0},{48,16},{64,32},{80,48},{96,64},{112,80},{128,96},{144,112}... | collective-permute-start | bytes 1572872 | tf_op jit(solution)/shard_map/ppermute | solution.py:12
  750.2 24.0 %collective-permute-start.8 = (f32[512,256]{1,0:T(8,128)S(1)}, f32[512,256]{1,0:T(8,128)S(1)}, u32[]{:S(2)}, u32[]{:S(2)}) collective-permute-start(f32[512,256]{1,0:T(8,128)S(1)} %fusion.34), channel_id=1, source_target_pairs={{0,32},{16,48},{32,64},{48,80},{64,96},{80,112},{96,128},{112,144}... | collective-permute-start | bytes 1572872 | tf_op jit(solution)/shard_map/ppermute | solution.py:12
  775.3 31.8 %copy-start.19 = (f32[512,32]{0,1:T(8,128)S(1)}, f32[512,32]{0,1:T(8,128)}, u32[]{:S(2)}) copy-start(f32[512,32]{0,1:T(8,128)} %convolution_negate_fusion.1) | copy-start | bytes 196612
  795.6 11.6 %copy-start.10 = (f32[512,512]{0,1:T(8,128)S(1)}, f32[512,512]{0,1:T(8,128)}, u32[]{:S(2)}) copy-start(f32[512,512]{0,1:T(8,128)} %all-gather.30.cloned.1.call-done) | copy-start | bytes 3145732
  798.7 12.8 %copy-start.18 = (f32[512,32]{0,1:T(8,128)S(1)}, f32[512,32]{0,1:T(8,128)}, u32[]{:S(2)}) copy-start(f32[512,32]{0,1:T(8,128)} %convolution_negate_fusion) | copy-start | bytes 196612
  798.7 151.0 %collective-permute-start.11 = (f32[512,256]{1,0:T(8,128)S(1)}, f32[512,256]{1,0:T(8,128)}, u32[]{:S(2)}, u32[]{:S(2)}) collective-permute-start(f32[512,256]{1,0:T(8,128)S(1)} %fusion.36), channel_id=1, source_target_pairs={{64,0},{80,16},{96,32},{112,48},{128,64},{144,80},{160,96},{176,11... | collective-permute-start | bytes 1572872 | tf_op jit(solution)/shard_map/ppermute | solution.py:12
  802.6 149.3 %collective-permute-start.10 = (f32[512,256]{1,0:T(8,128)S(1)}, f32[512,256]{1,0:T(8,128)}, u32[]{:S(2)}, u32[]{:S(2)}) collective-permute-start(f32[512,256]{1,0:T(8,128)S(1)} %fusion.36), channel_id=1, source_target_pairs={{0,64},{16,80},{32,96},{48,112},{64,128},{80,144},{96,160},{112,17... | collective-permute-start | bytes 1572872 | tf_op jit(solution)/shard_map/ppermute | solution.py:12
  807.9 63.7 %collective-permute-start.5 = (f32[1,512,32]{1,2,0:T(8,128)S(1)}, f32[1,512,32]{1,2,0:T(8,128)S(1)}, u32[]{:S(2)}, u32[]{:S(2)}) collective-permute-start(f32[1,512,32]{1,2,0:T(8,128)S(1)} %convolution_bitcast_fusion.2), channel_id=1, source_target_pairs={{64,0},{80,16},{96,32},{112,48},{128,64},{144,80},{160,96},{176,11... | collective-permute-start | bytes 196616 | tf_op jit(solution)/shard_map/ppermute | solution.py:12
  812.3 134.8 %copy-start.16 = (f32[512,32]{0,1:T(8,128)S(1)}, f32[512,32]{0,1:T(8,128)}, u32[]{:S(2)}) copy-start(f32[512,32]{0,1:T(8,128)} %fusion.7) | copy-start | bytes 196612
  812.3 134.8 %collective-permute-start.4 = (f32[1,512,32]{1,2,0:T(8,128)S(1)}, f32[1,512,32]{1,2,0:T(8,128)S(1)}, u32[]{:S(2)}, u32[]{:S(2)}) collective-permute-start(f32[1,512,32]{1,2,0:T(8,128)S(1)} %convolution_bitcast_fusion.3), channel_id=1, source_target_pairs={{0,64},{16,80},{32,96},{48,112},{64,128},{80,144},{96,160},{112,17... | collective-permute-start | bytes 196616 | tf_op jit(solution)/shard_map/ppermute | solution.py:12
  871.6 78.1 %copy-start.14 = (f32[512,512]{0,1:T(8,128)S(1)}, f32[512,512]{0,1:T(8,128)}, u32[]{:S(2)}) copy-start(f32[512,512]{0,1:T(8,128)} %all-gather.32.cloned.1.call-done) | copy-start | bytes 3145732
  949.7 2.3 copy-start.13
Sparse Core Ops, SparseCore 0:
  11.0 81.8 all-gather.33
  104.1 72.0 all-gather.15
  179.2 72.0 all-gather.37
  254.1 72.0 all-gather.35
  329.6 72.0 all-gather.19
  414.0 72.0 all-gather.21
  489.6 72.0 all-gather.23
  564.7 72.0 all-gather.17
  639.8 72.0 all-gather.27
  724.0 71.5 all-gather.29
  799.2 72.3 all-gather.31
  875.1 72.0 all-gather.25
where the time goes:
time: 965 us; the launch traced here: 962 us
  waiting for transfers between devices  820 us (85%)
  matrix products  54.2 us (6%)
  starting transfers between devices  45 us (5%)
  local copies, waits for them, and re-layouts  27.3 us (3%)
  between operations  14.8 us (2%)
    all_gather x3, waiting for transfers between devices, shards(): lax.all_gather(center, 'ch', axis=1, tiled=True)  230 us
    all_gather x3, waiting for transfers between devices, shards(): lax.all_gather(down_link, 'ch', axis=1, tiled=True)  220 us
    all_gather x3, waiting for transfers between devices, shards(): lax.all_gather(up_link, 'ch', axis=1, tiled=True)  187 us
    all_gather x3, waiting for transfers between devices, shards(): inverse = lax.all_gather(inverse_cols, 'ch', axis=1, tiled=True)  160 us
    dot_general x31, matrix products, product(): jnp.dot(left, right, precision=lax.Precision.HIGHEST, preferred_element_t...  54.2 us
    ppermute x12, starting transfers between devices, shifted(): return lax.ppermute(x, axis, pairs)  44.5 us
    gather x3, local copies, waits for them, and re-layouts, first_inverse(): diag_vals = jnp.diagonal(center)  26 us
    ppermute x12, waiting for transfers between devices, shifted(): return lax.ppermute(x, axis, pairs)  21.1 us
  transfers between devices with their start and end apart: 24, of which 16 were waited for; matrix products, arithmetic and copies ran while one was open for 4% of the time, Pallas kernels for 0%

commit v1 on v0

v1 whole, which is shorter than its diff:
```python
import functools

import jax
import jax.numpy as jnp
from jax import lax
from jax.experimental import pallas as pl
from jax.experimental.pallas import tpu as pltpu
from jax.sharding import PartitionSpec as P

LEVELS = 3
MESH = pl.DeviceIdType.MESH
F32 = jnp.float32
BF16 = jnp.bfloat16


def split(x):
    hi = x.astype(BF16)
    return hi, (x - hi.astype(F32)).astype(BF16)


def dot(a, b):
    return jnp.dot(a, b, preferred_element_type=F32)


def product(left, hi, lo):
    left_hi, left_lo = split(left)
    return dot(left_hi, hi) + (dot(left_lo, hi) + dot(left_hi, lo))


def kernel(sectors, m, a_in, l_in, u_in, b_in, a_out, b_out,
           wa, wl, wu, zm, zb, rm_dn, rm_up, rb_dn, rb_up, rs, source,
           inv_hi, inv_lo, l_hi, l_lo, u_hi, u_lo, load_sem, ssem, rsem):
    sec = lax.axis_index("sec")
    ch = lax.axis_index("ch")
    z, y = ch // 4, ch % 4
    ins = (a_in, l_in, u_in)
    whole = (wa, wl, wu)

    loads = [pltpu.make_async_copy(ins[i], whole[i].at[0, z, y], load_sem.at[i]) for i in range(3)]
    loads.append(pltpu.make_async_copy(b_in, rs, load_sem.at[3]))
    for load in loads:
        load.start()

    def zat(d):
        return (z + d) % 4

    def yat(d):
        return (y + d) % 4

    z_next, z_prev = (sec, zat(1) * 4 + y), (sec, zat(3) * 4 + y)
    y_next, y_prev, y_far = (sec, z * 4 + yat(1)), (sec, z * 4 + yat(3)), (sec, z * 4 + yat(2))
    strides = [2 ** k for k in range(LEVELS)]
    below = [sec - s >= 0 for s in strides]
    above = [sec + s < sectors for s in strides]

    barrier = pltpu.get_barrier_semaphore()
    for device in (z_next, z_prev, y_next, y_prev, y_far):
        pl.semaphore_signal(barrier, inc=1, device_id=device, device_id_type=MESH)
    for k, s in enumerate(strides):
        @pl.when(below[k])
        def _():
            pl.semaphore_signal(barrier, inc=1, device_id=(sec - s, ch), device_id_type=MESH)

        @pl.when(above[k])
        def _():
            pl.semaphore_signal(barrier, inc=1, device_id=(sec + s, ch), device_id_type=MESH)

    for k in range(LEVELS):
        @pl.when(jnp.logical_not(below[k]))
        def _():
            rm_dn[k] = jnp.zeros_like(rm_dn[k])
            rb_dn[k] = jnp.zeros_like(rb_dn[k])

        @pl.when(jnp.logical_not(above[k]))
        def _():
            rm_up[k] = jnp.zeros_like(rm_up[k])
            rb_up[k] = jnp.zeros_like(rb_up[k])

    for load in loads:
        load.wait()
    source[...] = rs[...].T

    peers = 5
    for k in range(LEVELS):
        peers = peers + below[k].astype(jnp.int32) + above[k].astype(jnp.int32)
    pl.semaphore_wait(barrier, peers)

    sent = []

    def copy(src, dst, index, device):
        return pltpu.make_async_remote_copy(
            src_ref=src, dst_ref=dst, send_sem=ssem.at[index], recv_sem=rsem.at[index],
            device_id=device, device_id_type=MESH)

    def push(ref, index, device):
        out = copy(ref, ref, index, device)
        out.start()
        sent.append(out)

    def arrived(ref, index):
        copy(ref, ref, index, y_next).wait_recv()

    def slab(i, dz, dy):
        return whole[i].at[0, zat(dz), yat(dy)]

    def half(i, dz, part):
        return whole[i].at[0, zat(dz), y, pl.ds(16 * part, 16)]

    def z_own(i):
        push(slab(i, 0, 0), 16 * i, z_next)
        push(slab(i, 0, 0), 16 * i + 1, z_prev)

    def y_send(i, r):
        push(slab(i, r, 0), 16 * i + 4 + r, y_next)
        push(slab(i, r, 0), 16 * i + 8 + r, y_prev)

    def z_relay(i):
        arrived(slab(i, 3, 0), 16 * i)
        push(half(i, 3, 0), 16 * i + 2, z_next)
        arrived(slab(i, 1, 0), 16 * i + 1)
        push(half(i, 1, 1), 16 * i + 3, z_prev)
        y_send(i, 3)
        y_send(i, 1)

    def z_last(i):
        arrived(half(i, 2, 0), 16 * i + 2)
        arrived(half(i, 2, 1), 16 * i + 3)
        y_send(i, 2)

    def y_relay(i, r):
        arrived(slab(i, r, 3), 16 * i + 4 + r)
        if r % 2 == 0:
            push(slab(i, r, 3), 16 * i + 12 + r, y_next)
        arrived(slab(i, r, 1), 16 * i + 8 + r)
        if r % 2 == 1:
            push(slab(i, r, 1), 16 * i + 12 + r, y_prev)

    def y_last(i):
        for r in range(4):
            arrived(slab(i, r, 2), 16 * i + 12 + r)

    z_own(0)
    z_own(1)
    y_send(0, 0)
    y_send(1, 0)
    y_send(2, 0)
    z_relay(0)
    z_own(2)
    y_relay(0, 0)
    y_relay(1, 0)
    y_relay(2, 0)
    y_relay(0, 1)
    y_relay(0, 3)
    z_relay(1)
    z_last(0)
    y_relay(1, 1)
    y_relay(1, 3)
    y_relay(0, 2)
    z_relay(2)
    z_last(1)
    y_relay(2, 1)
    y_relay(2, 3)

    def invert(k):
        block = wa[k].reshape(m, m)
        rows = lax.broadcasted_iota(jnp.int32, (m, m), 0)
        cols = lax.broadcasted_iota(jnp.int32, (m, m), 1)
        on = rows == cols
        diag = jnp.where(on, block, 0.0)
        across = 1.0 / jnp.sum(diag, axis=0, keepdims=True)
        down = 1.0 / jnp.sum(diag, axis=1, keepdims=True)
        start = jnp.where(on, across, -(down * block * across))
        block_hi, block_lo = split(block)
        start_hi, start_lo = split(start)
        inner = product(start, block_hi, block_lo)
        inverse = 2.0 * start - product(inner, start_hi, start_lo)
        inv_hi[...], inv_lo[...] = split(inverse)

    def y_arrived(i, k):
        base = 48 + 9 * (k - 1) + 3 * i
        arrived(whole[i].at[k, :, yat(3)], base)
        arrived(whole[i].at[k, :, yat(1)], base + 1)
        arrived(whole[i].at[k, :, yat(2)], base + 2)

    def y_push(i, k):
        base = 48 + 9 * (k - 1) + 3 * i
        push(whole[i].at[k, :, y], base, y_next)
        push(whole[i].at[k, :, y], base + 1, y_prev)
        push(whole[i].at[k, :, y], base + 2, y_far)

    shifts = []

    def shift(k, src_up, dst_up, src_dn, dst_dn, index):
        up = copy(src_up, dst_up, index, (sec + strides[k], ch))
        dn = copy(src_dn, dst_dn, index + 1, (sec - strides[k], ch))

        @pl.when(above[k])
        def _():
            up.start()

        @pl.when(below[k])
        def _():
            dn.start()

        shifts.append((k, up, dn))

    def shifted(k, dst_up, dst_dn, index):
        @pl.when(below[k])
        def _():
            arrived(dst_up, index)

        @pl.when(above[k])
        def _():
            arrived(dst_dn, index + 1)

    def update_source(k):
        shifted(k, rb_dn.at[k], rb_up.at[k], 66 + 4 * k + 2)
        source[...] = source[...] - product(rb_dn[k], l_hi[...], l_lo[...]) - product(rb_up[k], u_hi[...], u_lo[...])

    quarter = m // 4
    for k in range(LEVELS):
        index = 66 + 4 * k
        if k == 0:
            y_last(0)
        else:
            y_arrived(0, k)
        invert(k)
        if k == 0:
            y_relay(1, 2)
            z_last(2)
            y_relay(2, 2)
        if k == LEVELS - 1:
            zm[k, 0:32] = product(wl[k, z, y], inv_hi[...], inv_lo[...])
            zm[k, 32:64] = product(wu[k, z, y], inv_hi[...], inv_lo[...])
            shift(k, zm.at[k, pl.ds(32, 32)], rm_dn.at[k, pl.ds(32, 32)],
                  zm.at[k, pl.ds(0, 32)], rm_up.at[k, pl.ds(0, 32)], index)
        else:
            zm[k, 0:quarter] = product(wl[k, :, y].reshape(quarter, m), inv_hi[...], inv_lo[...])
            zm[k, quarter:] = product(wu[k, :, y].reshape(quarter, m), inv_hi[...], inv_lo[...])
            shift(k, zm.at[k], rm_dn.at[k], zm.at[k], rm_up.at[k], index)
        if k > 0:
            update_source(k - 1)
        zb[k] = product(source[...], inv_hi[...], inv_lo[...])
        shift(k, zb.at[k], rb_dn.at[k], zb.at[k], rb_up.at[k], index + 2)
        if k == 0:
            y_last(1)
            y_last(2)
        else:
            y_arrived(1, k)
            y_arrived(2, k)
        l_hi[...], l_lo[...] = split(wl[k].reshape(m, m))
        u_hi[...], u_lo[...] = split(wu[k].reshape(m, m))
        if k == LEVELS - 1:
            shifted(k, rm_dn.at[k, pl.ds(32, 32)], rm_up.at[k, pl.ds(0, 32)], index)
            a_out[...] = (wa[k, z, y] - product(rm_dn[k, 32:64], l_hi[...], l_lo[...])
                          - product(rm_up[k, 0:32], u_hi[...], u_lo[...]))
        else:
            shifted(k, rm_dn.at[k], rm_up.at[k], index)
            from_dn = product(rm_dn[k], l_hi[...], l_lo[...])
            from_up = product(rm_up[k], u_hi[...], u_lo[...])
            center = wa[k, :, y].reshape(quarter, m) - from_dn[quarter:] - from_up[:quarter]
            wa[k + 1, :, y] = center.reshape(4, quarter // 4, m)
            y_push(0, k + 1)
            wl[k + 1, :, y] = (-from_dn[:quarter]).reshape(4, quarter // 4, m)
            y_push(1, k + 1)
            wu[k + 1, :, y] = (-from_up[quarter:]).reshape(4, quarter // 4, m)
            y_push(2, k + 1)
    update_source(LEVELS - 1)
    b_out[...] = source[...].T

    for out in sent:
        out.wait_send()
    for k, up, dn in shifts:
        @pl.when(above[k])
        def _():
            up.wait_send()

        @pl.when(below[k])
        def _():
            dn.wait_send()


def shards(sectors, diag_blocks, lower_blocks, upper_blocks, sources):
    m = diag_blocks.shape[1]
    width = diag_blocks.shape[2]
    columns = sources.shape[2]
    quarter = m // 4
    copies = 66 + 4 * LEVELS
    vmem = pl.BlockSpec(memory_space=pltpu.VMEM)
    hbm = pl.BlockSpec(memory_space=pl.ANY)
    center, source = pl.pallas_call(
        functools.partial(kernel, sectors, m),
        out_shape=(jax.ShapeDtypeStruct((width, m), F32), jax.ShapeDtypeStruct((m, columns), F32)),
        in_specs=[hbm] * 4,
        out_specs=(vmem, vmem),
        scratch_shapes=[
            pltpu.VMEM((LEVELS, 4, 4, width, m), F32),
            pltpu.VMEM((LEVELS, 4, 4, width, m), F32),
            pltpu.VMEM((LEVELS, 4, 4, width, m), F32),
            pltpu.VMEM((LEVELS, 2 * quarter, m), F32),
            pltpu.VMEM((LEVELS, columns, m), F32),
            pltpu.VMEM((LEVELS, 2 * quarter, m), F32),
            pltpu.VMEM((LEVELS, 2 * quarter, m), F32),
            pltpu.VMEM((LEVELS, columns, m), F32),
            pltpu.VMEM((LEVELS, columns, m), F32),
            pltpu.VMEM((m, columns), F32),
            pltpu.VMEM((columns, m), F32),
            pltpu.VMEM((m, m), BF16),
            pltpu.VMEM((m, m), BF16),
            pltpu.VMEM((m, m), BF16),
            pltpu.VMEM((m, m), BF16),
            pltpu.VMEM((m, m), BF16),
            pltpu.VMEM((m, m), BF16),
            pltpu.SemaphoreType.DMA((4,)),
            pltpu.SemaphoreType.DMA((copies,)),
            pltpu.SemaphoreType.DMA((copies,)),
        ],
        compiler_params=pltpu.CompilerParams(
            collective_id=0, has_side_effects=True, vmem_limit_bytes=56 * 2**20),
        name="reduction",
    )(diag_blocks[0].T, lower_blocks[0].T, upper_blocks[0].T, sources[0])
    return center.T[None], source[None]


def solution(mesh):
    placed = P("sec", None, "ch")
    return jax.shard_map(
        functools.partial(shards, mesh.shape["sec"]),
        mesh=mesh,
        in_specs=(placed,) * 4,
        out_specs=(placed, placed),
        check_vma=False,
    )
```

time: 965 us -> 143 us (0.15)
  the two profiles are of different devices: /device:TPU:6 before, /device:TPU:59 now
where the time goes in v1:
time: 143 us
  Pallas kernels  139 us (97%)
  local copies, waits for them, and re-layouts  3.34 us (2%)
    pallas_call x1, Pallas kernels, shards(): pl.pallas_call(functools.partial(kernel, sectors, m), out_shape=(jax.Shap...  139 us
    unnamed x2, local copies, waits for them, and re-layouts  3.34 us

profile of v1, /device:TPU:59, one launch (start us, length us, event | category | flops | bytes accessed | tf_op | source)
XLA Modules:
  0.0 143.1 jit_solution(5480268924743992685)
XLA Ops:
  0.6 139.2 %reduction.1 = (f32[32,512]{1,0:T(8,128)}, f32[512,256]{1,0:T(8,128)}) custom-call(f32[32,512]{1,0:T(8,128)} %bitcast.17, f32[32,512]{1,0:T(8,128)} %bitcast.18, f32[32,512]{1,0:T(8,128)} %bitcast.19, f32[512,256]{1,0:T(8,128)} %bitcast.14), custom_call_target="tpu_custom_call" | custom-call | tf_op jit(solution)/shard_map/reduction/pallas_call | solution.py:291
  139.8 1.5 %copy.8 = f32[1,512,32]{1,2,0:T(8,128)} copy(f32[1,512,32]{1,2,0:T(8,128)} %bitcast.16) | data formatting | bytes 131072
  141.3 1.9 %copy.9 = f32[1,512,256]{2,1,0:T(8,128)} copy(f32[1,512,256]{2,1,0:T(8,128)} %bitcast.15) | data formatting | bytes 1048576

commit v2 on v0

v2 whole, which is shorter than its diff:
```python
import functools

import jax
import jax.numpy as jnp
from jax import lax
from jax.experimental import pallas as pl
from jax.experimental.pallas import tpu as pltpu
from jax.sharding import PartitionSpec as P

LEVELS = 3
NEAR, FAR = 0, 1
MESH = pl.DeviceIdType.MESH
F32 = jnp.float32
BF16 = jnp.bfloat16


def split(x):
    hi = x.astype(BF16)
    return hi, (x - hi.astype(F32)).astype(BF16)


def dot(a, b):
    return jnp.dot(a, b, preferred_element_type=F32)


def product(left, hi, lo):
    left_hi, left_lo = split(left)
    return dot(left_hi, hi) + (dot(left_lo, hi) + dot(left_hi, lo))


class Slots:
    def __init__(self):
        self.taken = {}

    def __call__(self, *name):
        return self.taken.setdefault(name, len(self.taken))


def kernel(sectors, m, a_in, l_in, u_in, b_in, a_out, b_out,
           wa, wc, zq, zwhole, rwhole, rq, zb, rb, b_raw, source,
           inv_hi, inv_lo, c_hi, c_lo, load_sem, ssem, rsem):
    sec = lax.axis_index("sec")
    ch = lax.axis_index("ch")
    z, y = ch // 4, ch % 4
    core = sec % 2
    toward = 1 - 2 * core
    side = 1 - 2 * ((sec % 8) // 4)
    quarter = m // 4
    half_rows = source.shape[0] // 2
    chunk = source.shape[0] // 4

    loads = [
        pltpu.make_async_copy(a_in, wa.at[0, z, y], load_sem.at[0]),
        pltpu.make_async_copy(l_in, wc.at[1 - core, 0, z, y], load_sem.at[1]),
        pltpu.make_async_copy(u_in, wc.at[core, 0, z, y], load_sem.at[2]),
        pltpu.make_async_copy(b_in, b_raw, load_sem.at[3]),
    ]
    for load in loads:
        load.start()

    def zat(d):
        return (z + d) % 4

    def yat(d):
        return (y + d) % 4

    def inside(index):
        return jnp.logical_and(index >= 0, index < sectors)

    z_next, z_prev = (sec, zat(1) * 4 + y), (sec, zat(3) * 4 + y)
    y_next, y_prev, y_far = (sec, z * 4 + yat(1)), (sec, z * 4 + yat(3)), (sec, z * 4 + yat(2))
    near = [sec + toward * 2 ** k for k in range(LEVELS)]
    far = [sec - toward * 2 ** k for k in range(LEVELS)]
    has_near = [inside(i) for i in near]
    has_far = [inside(i) for i in far]
    mirror, onward, backward = sec + 4 * side, sec + 8 * side, sec - 8 * side
    has_onward, has_backward = inside(onward), inside(backward)

    barrier = pltpu.get_barrier_semaphore()

    def greet(device):
        pl.semaphore_signal(barrier, inc=1, device_id=device, device_id_type=MESH)

    for device in (z_next, z_prev, y_next, y_prev, y_far):
        greet(device)
    peers = 5
    for index, there in zip(near + far + [onward, backward], has_near + has_far + [has_onward, has_backward]):
        @pl.when(there)
        def _():
            greet((index, ch))

        peers = peers + there.astype(jnp.int32)
    pl.semaphore_wait(barrier, peers)
    for load in loads:
        load.wait()

    slots = Slots()
    sent = []

    def copy(src, dst, index, device):
        return pltpu.make_async_remote_copy(
            src_ref=src, dst_ref=dst, send_sem=ssem.at[index], recv_sem=rsem.at[index],
            device_id=device, device_id_type=MESH)

    def push(ref, name, device):
        out = copy(ref, ref, slots(*name), device)
        out.start()
        sent.append((None, out))

    def arrived(ref, name):
        copy(ref, ref, slots(*name), y_next).wait_recv()

    def shift(there, src, dst, name, target):
        out = copy(src, dst, slots(*name), (target, ch))

        @pl.when(there)
        def _():
            out.start()

        sent.append((there, out))

    def shifted(there, ref, name):
        @pl.when(there)
        def _():
            arrived(ref, name)

    whole = (wa.at[0], wc.at[FAR, 0], wc.at[NEAR, 0])

    def slab(i, dz, dy):
        return whole[i].at[zat(dz), yat(dy)]

    def half(i, dz, part):
        return whole[i].at[zat(dz), y, pl.ds(16 * part, 16)]

    def z_own(i):
        push(slab(i, 0, 0), ("z", i, 1), z_next)
        push(slab(i, 0, 0), ("z", i, 3), z_prev)

    def y_send(i, r):
        push(slab(i, r, 0), ("y", i, r, 1), y_next)
        push(slab(i, r, 0), ("y", i, r, 3), y_prev)

    def z_relay(i):
        arrived(slab(i, 3, 0), ("z", i, 1))
        push(half(i, 3, 0), ("zz", i, 1), z_next)
        arrived(slab(i, 1, 0), ("z", i, 3))
        push(half(i, 1, 1), ("zz", i, 3), z_prev)
        y_send(i, 3)
        y_send(i, 1)

    def z_last(i):
        arrived(half(i, 2, 0), ("zz", i, 1))
        arrived(half(i, 2, 1), ("zz", i, 3))
        y_send(i, 2)

    def y_relay(i, r):
        arrived(slab(i, r, 3), ("y", i, r, 1))
        if r % 2 == 0:
            push(slab(i, r, 3), ("yy", i, r), y_next)
        arrived(slab(i, r, 1), ("y", i, r, 3))
        if r % 2 == 1:
            push(slab(i, r, 1), ("yy", i, r), y_prev)

    def y_last(i):
        for r in range(4):
            arrived(slab(i, r, 2), ("yy", i, r))

    def part(ref, dy, p):
        return ref.at[pl.ds(2 * p, 2), yat(dy)]

    def ring_start(ref, k):
        push(part(ref, 0, 0), ("r", k, 0), y_next)
        push(part(ref, 0, 1), ("r", k, 1), y_prev)
        push(part(ref, 0, 1), ("r", k, 2), y_next)
        push(part(ref, 0, 0), ("r", k, 3), y_prev)

    def ring_relay(ref, k):
        arrived(part(ref, 3, 0), ("r", k, 0))
        push(part(ref, 3, 0), ("r", k, 4), y_next)
        arrived(part(ref, 1, 1), ("r", k, 1))
        push(part(ref, 1, 1), ("r", k, 5), y_prev)

    def ring_end(ref, k):
        arrived(part(ref, 3, 1), ("r", k, 2))
        arrived(part(ref, 1, 0), ("r", k, 3))
        arrived(part(ref, 2, 0), ("r", k, 4))
        arrived(part(ref, 2, 1), ("r", k, 5))

    def spread(ref, k, role):
        push(ref.at[:, y], ("s", k, role, 1), y_next)
        push(ref.at[:, y], ("s", k, role, 3), y_prev)
        push(ref.at[:, y], ("s", k, role, 2), y_far)

    def spread_end(ref, k, role):
        arrived(ref.at[:, yat(3)], ("s", k, role, 1))
        arrived(ref.at[:, yat(1)], ("s", k, role, 3))
        arrived(ref.at[:, yat(2)], ("s", k, role, 2))

    def rows(ref):
        return ref[...].reshape(m, m)

    def own(ref):
        return ref[:, y].reshape(quarter, m)

    def put(ref, value):
        ref[:, y] = value.reshape(4, quarter // 4, m)

    def invert(k):
        block = rows(wa.at[k])
        on = lax.broadcasted_iota(jnp.int32, (m, m), 0) == lax.broadcasted_iota(jnp.int32, (m, m), 1)
        diag = jnp.where(on, block, 0.0)
        across = 1.0 / jnp.sum(diag, axis=0, keepdims=True)
        down = 1.0 / jnp.sum(diag, axis=1, keepdims=True)
        start = jnp.where(on, across, -(down * block * across))
        block_hi, block_lo = split(block)
        start_hi, start_lo = split(start)
        inner = product(start, block_hi, block_lo)
        inv_hi[...], inv_lo[...] = split(2.0 * start - product(inner, start_hi, start_lo))

    def solve(value):
        return product(value, inv_hi[...], inv_lo[...])

    def couple(value, role):
        return product(value, c_hi[role], c_lo[role])

    def hold(k, role):
        c_hi[role], c_lo[role] = split(rows(wc.at[role, k]))

    def update_source(k):
        shifted(has_near[k], rb.at[k, NEAR], ("b", k, NEAR))
        shifted(has_far[k], rb.at[k, FAR], ("b", k, FAR))
        source[...] = source[...] - couple(rb[k, NEAR], NEAR) - couple(rb[k, FAR], FAR)

    z_own(0)
    z_own(1)
    y_send(0, 0)
    y_send(1, 0)
    y_send(2, 0)
    source[...] = b_raw[...].T

    def clear(there, ref):
        @pl.when(jnp.logical_not(there))
        def _():
            ref[...] = jnp.zeros_like(ref)

    clear(has_far[0], rq.at[0, FAR])
    clear(has_far[0], rb.at[0, FAR])
    for k in range(1, LEVELS):
        clear(has_near[k], rq.at[k, NEAR])
        clear(has_far[k], rq.at[k, FAR])
    clear(has_near[1], rb.at[1, NEAR])
    clear(has_far[1], rb.at[1, FAR])
    clear(has_backward, rb.at[2, 1])
    z_relay(0)
    z_own(2)
    y_relay(0, 0)
    y_relay(1, 0)
    y_relay(2, 0)
    y_relay(0, 1)
    y_relay(0, 3)
    z_relay(1)
    z_last(0)
    y_relay(1, 1)
    y_relay(1, 3)
    y_relay(0, 2)
    z_relay(2)
    z_last(1)
    y_relay(2, 1)
    y_relay(2, 3)

    y_last(0)
    invert(0)
    y_relay(1, 2)
    z_last(2)
    y_relay(2, 2)
    zq[0, FAR] = solve(own(wc.at[FAR, 0]))
    shift(has_far[0], zq.at[0, FAR], rq.at[0, FAR, FAR], ("q", 0, FAR, FAR), far[0])
    zq[0, NEAR] = solve(own(wc.at[NEAR, 0]))
    shift(has_near[0], zq.at[0, NEAR], rq.at[0, NEAR, NEAR], ("q", 0, NEAR, NEAR), near[0])
    shift(has_far[0], zq.at[0, NEAR], rq.at[0, FAR, NEAR], ("q", 0, FAR, NEAR), far[0])
    zb[0] = solve(source[...])
    shift(has_far[0], zb.at[0], rb.at[0, FAR], ("b", 0, FAR), far[0])
    shift(has_near[0], zb.at[0], rb.at[0, NEAR], ("b", 0, NEAR), near[0])
    y_last(1)
    hold(0, FAR)
    shifted(has_far[0], rq.at[0, FAR, FAR], ("q", 0, FAR, FAR))
    center = own(wa.at[0]) - couple(rq[0, FAR, FAR], FAR)
    y_last(2)
    hold(0, NEAR)
    shifted(has_near[0], rq.at[0, NEAR, NEAR], ("q", 0, NEAR, NEAR))
    put(wa.at[1], center - couple(rq[0, NEAR, NEAR], NEAR))
    ring_start(wa.at[1], 1)
    zwhole[...] = solve(rows(wc.at[FAR, 0]))
    shift(has_near[0], zwhole, rwhole, ("w",), near[0])
    shifted(has_far[0], rq.at[0, FAR, NEAR], ("q", 0, FAR, NEAR))
    put(wc.at[FAR, 1], -couple(rq[0, FAR, NEAR], FAR))
    ring_relay(wa.at[1], 1)
    spread(wc.at[FAR, 1], 1, FAR)
    shifted(has_near[0], rwhole, ("w",))
    wc[NEAR, 1] = (-couple(rwhole[...], NEAR)).reshape(4, 4, quarter // 4, m)
    update_source(0)

    ring_end(wa.at[1], 1)
    invert(1)
    zq[1, NEAR] = solve(own(wc.at[NEAR, 1]))
    shift(has_near[1], zq.at[1, NEAR], rq.at[1, FAR, NEAR], ("q", 1, FAR, NEAR), near[1])
    zq[1, FAR] = solve(own(wc.at[FAR, 1]))
    shift(has_far[1], zq.at[1, FAR], rq.at[1, NEAR, FAR], ("q", 1, NEAR, FAR), far[1])
    shift(has_near[1], zq.at[1, FAR], rq.at[1, FAR, FAR], ("q", 1, FAR, FAR), near[1])
    shift(has_far[1], zq.at[1, NEAR], rq.at[1, NEAR, NEAR], ("q", 1, NEAR, NEAR), far[1])
    zb[1] = solve(source[...])
    shift(has_near[1], zb.at[1], rb.at[1, FAR], ("b", 1, FAR), near[1])
    shift(has_far[1], zb.at[1], rb.at[1, NEAR], ("b", 1, NEAR), far[1])
    hold(1, NEAR)
    spread_end(wc.at[FAR, 1], 1, FAR)
    hold(1, FAR)
    shifted(has_near[1], rq.at[1, NEAR, FAR], ("q", 1, NEAR, FAR))
    shifted(has_far[1], rq.at[1, FAR, NEAR], ("q", 1, FAR, NEAR))
    put(wa.at[2], own(wa.at[1]) - couple(rq[1, NEAR, FAR], NEAR) - couple(rq[1, FAR, NEAR], FAR))
    ring_start(wa.at[2], 2)
    shifted(has_near[1], rq.at[1, NEAR, NEAR], ("q", 1, NEAR, NEAR))
    put(wc.at[NEAR, 2], -couple(rq[1, NEAR, NEAR], NEAR))
    shifted(has_far[1], rq.at[1, FAR, FAR], ("q", 1, FAR, FAR))
    put(wc.at[FAR, 2], -couple(rq[1, FAR, FAR], FAR))
    ring_relay(wa.at[2], 2)
    spread(wc.at[NEAR, 2], 2, NEAR)
    spread(wc.at[FAR, 2], 2, FAR)

    ring_end(wa.at[2], 2)
    invert(2)
    zq[2, NEAR, 0:32] = solve(wc[NEAR, 2, z, y])
    shift(has_near[2], zq.at[2, NEAR, pl.ds(0, 32)], rq.at[2, FAR, NEAR, pl.ds(0, 32)], ("q", 2, FAR), near[2])
    zq[2, FAR, 0:32] = solve(wc[FAR, 2, z, y])
    shift(has_far[2], zq.at[2, FAR, pl.ds(0, 32)], rq.at[2, NEAR, FAR, pl.ds(0, 32)], ("q", 2, NEAR), far[2])
    update_source(1)
    always = mirror >= 0
    for c in range(4):
        if c % 2 == 0:
            here = pl.ds(chunk * c, half_rows)
            zb[2, here] = solve(source[here])
        here = pl.ds(chunk * c, chunk)
        shift(always, zb.at[2, here], rb.at[2, 0, here], ("c", c), mirror)
    spread_end(wc.at[NEAR, 2], 2, NEAR)
    hold(2, NEAR)
    spread_end(wc.at[FAR, 2], 2, FAR)
    hold(2, FAR)
    shifted(has_near[2], rq.at[2, NEAR, FAR, pl.ds(0, 32)], ("q", 2, NEAR))
    shifted(has_far[2], rq.at[2, FAR, NEAR, pl.ds(0, 32)], ("q", 2, FAR))
    a_out[...] = wa[2, z, y] - couple(rq[2, NEAR, FAR, 0:32], NEAR) - couple(rq[2, FAR, NEAR, 0:32], FAR)
    direct = (1 - toward * side) // 2
    for c in range(4):
        here = pl.ds(chunk * c, chunk)
        arrived(rb.at[2, 0, here], ("c", c))
        shift(has_onward, rb.at[2, 0, here], rb.at[2, 1, here], ("d", c), onward)
        if c % 2 == 1:
            here = pl.ds(chunk * (c - 1), half_rows)
            source[here] = source[here] - couple(rb[2, 0, here], direct)
    for c in range(4):
        shifted(has_backward, rb.at[2, 1, pl.ds(chunk * c, chunk)], ("d", c))
        if c % 2 == 1:
            here = pl.ds(chunk * (c - 1), half_rows)
            source[here] = source[here] - couple(rb[2, 1, here], 1 - direct)
    b_out[...] = source[...].T

    for there, out in sent:
        if there is None:
            out.wait_send()
        else:
            pl.when(there)(out.wait_send)


def shards(sectors, diag_blocks, lower_blocks, upper_blocks, sources):
    m = diag_blocks.shape[1]
    width = diag_blocks.shape[2]
    columns = sources.shape[2]
    quarter = m // 4
    copies = 128
    vmem = pl.BlockSpec(memory_space=pltpu.VMEM)
    hbm = pl.BlockSpec(memory_space=pl.ANY)
    center, source = pl.pallas_call(
        functools.partial(kernel, sectors, m),
        out_shape=(jax.ShapeDtypeStruct((width, m), F32), jax.ShapeDtypeStruct((m, columns), F32)),
        in_specs=[hbm] * 4,
        out_specs=(vmem, vmem),
        scratch_shapes=[
            pltpu.VMEM((LEVELS, 4, 4, width, m), F32),
            pltpu.VMEM((2, LEVELS, 4, 4, width, m), F32),
            pltpu.VMEM((LEVELS, 2, quarter, m), F32),
            pltpu.VMEM((m, m), F32),
            pltpu.VMEM((m, m), F32),
            pltpu.VMEM((LEVELS, 2, 2, quarter, m), F32),
            pltpu.VMEM((LEVELS, columns, m), F32),
            pltpu.VMEM((LEVELS, 2, columns, m), F32),
            pltpu.VMEM((m, columns), F32),
            pltpu.VMEM((columns, m), F32),
            pltpu.VMEM((m, m), BF16),
            pltpu.VMEM((m, m), BF16),
            pltpu.VMEM((2, m, m), BF16),
            pltpu.VMEM((2, m, m), BF16),
            pltpu.SemaphoreType.DMA((4,)),
            pltpu.SemaphoreType.DMA((copies,)),
            pltpu.SemaphoreType.DMA((copies,)),
        ],
        compiler_params=pltpu.CompilerParams(
            collective_id=0, has_side_effects=True, vmem_limit_bytes=56 * 2**20),
        name="reduction",
    )(diag_blocks[0].T, lower_blocks[0].T, upper_blocks[0].T, sources[0])
    return center.T[None], source[None]


def solution(mesh):
    placed = P("sec", None, "ch")
    return jax.shard_map(
        functools.partial(shards, mesh.shape["sec"]),
        mesh=mesh,
        in_specs=(placed,) * 4,
        out_specs=(placed, placed),
        check_vma=False,
    )
```

time: 965 us -> 136 us (0.14)
  waiting for transfers between devices: 820 us -> 0 us
  Pallas kernels: 0 us -> 131 us
  matrix products: 54.2 us -> 0 us
  starting transfers between devices: 45 us -> 0 us
  local copies, waits for them, and re-layouts: 27.3 us -> 3.34 us
  between operations: 14.8 us -> 0.64 us
    all_gather x12 -> x0, waiting for transfers between devices: 797 us -> none  [the longest x3 230 us: shards(): lax.all_gather(center, 'ch', axis=1, tiled=True)]
    pallas_call x0 -> x1, Pallas kernels: none -> 131 us  [shards(): pl.pallas_call(functools.partial(kernel, sectors, m), out_shape=(jax.Shap...]
    dot_general x31 -> x0, matrix products: 54.2 us -> none  [product(): jnp.dot(left, right, precision=lax.Precision.HIGHEST, preferred_element_t...]
    ppermute x12 -> x0, starting transfers between devices: 44.5 us -> none  [shifted(): return lax.ppermute(x, axis, pairs)]
    gather x3 -> x0, local copies, waits for them, and re-layouts: 26 us -> none  [first_inverse(): diag_vals = jnp.diagonal(center)]
    ppermute x12 -> x0, waiting for transfers between devices: 21.1 us -> none  [shifted(): return lax.ppermute(x, axis, pairs)]
  transfers between devices with their start and end apart: 24 -> 0, of which waited for: 16 -> 0; matrix products, arithmetic and copies ran while one was open for 4% -> 0% of each run, Pallas kernels for 0% -> 0%
where the time goes in v2:
time: 136 us; the launch traced here: 135 us
  Pallas kernels  131 us (96%)
  local copies, waits for them, and re-layouts  3.34 us (2%)
    pallas_call x1, Pallas kernels, shards(): pl.pallas_call(functools.partial(kernel, sectors, m), out_shape=(jax.Shap...  131 us
    unnamed x2, local copies, waits for them, and re-layouts  3.34 us

profile of v2, /device:TPU:6, one launch (start us, length us, event | category | flops | bytes accessed | tf_op | source)
XLA Modules:
  0.0 135.4 jit_solution(3900864566318525117)
XLA Ops:
  0.6 131.4 %reduction.1 = (f32[32,512]{1,0:T(8,128)}, f32[512,256]{1,0:T(8,128)}) custom-call(f32[32,512]{1,0:T(8,128)} %bitcast.17, f32[32,512]{1,0:T(8,128)} %bitcast.18, f32[32,512]{1,0:T(8,128)} %bitcast.19, f32[512,256]{1,0:T(8,128)} %bitcast.14), custom_call_target="tpu_custom_call" | custom-call | tf_op jit(solution)/shard_map/reduction/pallas_call | solution.py:380
  132.0 1.5 %copy.8 = f32[1,512,32]{1,2,0:T(8,128)} copy(f32[1,512,32]{1,2,0:T(8,128)} %bitcast.16) | data formatting | bytes 131072
  133.5 1.9 %copy.9 = f32[1,512,256]{2,1,0:T(8,128)} copy(f32[1,512,256]{2,1,0:T(8,128)} %bitcast.15) | data formatting | bytes 1048576

commit v3 on v2

--- a/solution.py
+++ b/solution.py
@@ -139,6 +139,7 @@
     def y_send(i, r):
         push(slab(i, r, 0), ("y", i, r, 1), y_next)
         push(slab(i, r, 0), ("y", i, r, 3), y_prev)
+        push(slab(i, r, 0), ("y", i, r, 2), y_far)
 
     def z_relay(i):
         arrived(slab(i, 3, 0), ("z", i, 1))
@@ -153,48 +154,32 @@
         arrived(half(i, 2, 1), ("zz", i, 3))
         y_send(i, 2)
 
-    def y_relay(i, r):
-        arrived(slab(i, r, 3), ("y", i, r, 1))
-        if r % 2 == 0:
-            push(slab(i, r, 3), ("yy", i, r), y_next)
-        arrived(slab(i, r, 1), ("y", i, r, 3))
-        if r % 2 == 1:
-            push(slab(i, r, 1), ("yy", i, r), y_prev)
-
     def y_last(i):
         for r in range(4):
-            arrived(slab(i, r, 2), ("yy", i, r))
+            arrived(slab(i, r, 3), ("y", i, r, 1))
+            arrived(slab(i, r, 1), ("y", i, r, 3))
+            arrived(slab(i, r, 2), ("y", i, r, 2))
 
     def part(ref, dy, p):
         return ref.at[pl.ds(2 * p, 2), yat(dy)]
 
-    def ring_start(ref, k):
-        push(part(ref, 0, 0), ("r", k, 0), y_next)
-        push(part(ref, 0, 1), ("r", k, 1), y_prev)
-        push(part(ref, 0, 1), ("r", k, 2), y_next)
-        push(part(ref, 0, 0), ("r", k, 3), y_prev)
-
-    def ring_relay(ref, k):
-        arrived(part(ref, 3, 0), ("r", k, 0))
-        push(part(ref, 3, 0), ("r", k, 4), y_next)
-        arrived(part(ref, 1, 1), ("r", k, 1))
-        push(part(ref, 1, 1), ("r", k, 5), y_prev)
-
-    def ring_end(ref, k):
-        arrived(part(ref, 3, 1), ("r", k, 2))
-        arrived(part(ref, 1, 0), ("r", k, 3))
-        arrived(part(ref, 2, 0), ("r", k, 4))
-        arrived(part(ref, 2, 1), ("r", k, 5))
-
-    def spread(ref, k, role):
-        push(ref.at[:, y], ("s", k, role, 1), y_next)
-        push(ref.at[:, y], ("s", k, role, 3), y_prev)
-        push(ref.at[:, y], ("s", k, role, 2), y_far)
-
-    def spread_end(ref, k, role):
-        arrived(ref.at[:, yat(3)], ("s", k, role, 1))
-        arrived(ref.at[:, yat(1)], ("s", k, role, 3))
-        arrived(ref.at[:, yat(2)], ("s", k, role, 2))
+    def ring_start(ref, *tag):
+        push(part(ref, 0, 0), ("r", *tag, 0), y_next)
+        push(part(ref, 0, 1), ("r", *tag, 1), y_prev)
+        push(part(ref, 0, 1), ("r", *tag, 2), y_next)
+        push(part(ref, 0, 0), ("r", *tag, 3), y_prev)
+
+    def ring_relay(ref, *tag):
+        arrived(part(ref, 3, 0), ("r", *tag, 0))
+        push(part(ref, 3, 0), ("r", *tag, 4), y_next)
+        arrived(part(ref, 1, 1), ("r", *tag, 1))
+        push(part(ref, 1, 1), ("r", *tag, 5), y_prev)
+
+    def ring_end(ref, *tag):
+        arrived(part(ref, 3, 1), ("r", *tag, 2))
+        arrived(part(ref, 1, 0), ("r", *tag, 3))
+        arrived(part(ref, 2, 0), ("r", *tag, 4))
+        arrived(part(ref, 2, 1), ("r", *tag, 5))
 
     def rows(ref):
         return ref[...].reshape(m, m)
@@ -226,11 +211,6 @@
     def hold(k, role):
         c_hi[role], c_lo[role] = split(rows(wc.at[role, k]))
 
-    def update_source(k):
-        shifted(has_near[k], rb.at[k, NEAR], ("b", k, NEAR))
-        shifted(has_far[k], rb.at[k, FAR], ("b", k, FAR))
-        source[...] = source[...] - couple(rb[k, NEAR], NEAR) - couple(rb[k, FAR], FAR)
-
     z_own(0)
     z_own(1)
     y_send(0, 0)
@@ -253,78 +233,77 @@
     clear(has_backward, rb.at[2, 1])
     z_relay(0)
     z_own(2)
-    y_relay(0, 0)
-    y_relay(1, 0)
-    y_relay(2, 0)
-    y_relay(0, 1)
-    y_relay(0, 3)
     z_relay(1)
     z_last(0)
-    y_relay(1, 1)
-    y_relay(1, 3)
-    y_relay(0, 2)
     z_relay(2)
     z_last(1)
-    y_relay(2, 1)
-    y_relay(2, 3)
+    z_last(2)
 
     y_last(0)
     invert(0)
-    y_relay(1, 2)
-    z_last(2)
-    y_relay(2, 2)
     zq[0, FAR] = solve(own(wc.at[FAR, 0]))
     shift(has_far[0], zq.at[0, FAR], rq.at[0, FAR, FAR], ("q", 0, FAR, FAR), far[0])
     zq[0, NEAR] = solve(own(wc.at[NEAR, 0]))
     shift(has_near[0], zq.at[0, NEAR], rq.at[0, NEAR, NEAR], ("q", 0, NEAR, NEAR), near[0])
-    shift(has_far[0], zq.at[0, NEAR], rq.at[0, FAR, NEAR], ("q", 0, FAR, NEAR), far[0])
     zb[0] = solve(source[...])
-    shift(has_far[0], zb.at[0], rb.at[0, FAR], ("b", 0, FAR), far[0])
-    shift(has_near[0], zb.at[0], rb.at[0, NEAR], ("b", 0, NEAR), near[0])
     y_last(1)
     hold(0, FAR)
     shifted(has_far[0], rq.at[0, FAR, FAR], ("q", 0, FAR, FAR))
+    shift(has_far[0], zq.at[0, NEAR], rq.at[0, FAR, NEAR], ("q", 0, FAR, NEAR), far[0])
     center = own(wa.at[0]) - couple(rq[0, FAR, FAR], FAR)
     y_last(2)
     hold(0, NEAR)
     shifted(has_near[0], rq.at[0, NEAR, NEAR], ("q", 0, NEAR, NEAR))
     put(wa.at[1], center - couple(rq[0, NEAR, NEAR], NEAR))
     ring_start(wa.at[1], 1)
+    shift(has_far[0], zb.at[0], rb.at[0, FAR], ("b", 0, FAR), far[0])
+    shift(has_near[0], zb.at[0], rb.at[0, NEAR], ("b", 0, NEAR), near[0])
     zwhole[...] = solve(rows(wc.at[FAR, 0]))
     shift(has_near[0], zwhole, rwhole, ("w",), near[0])
     shifted(has_far[0], rq.at[0, FAR, NEAR], ("q", 0, FAR, NEAR))
     put(wc.at[FAR, 1], -couple(rq[0, FAR, NEAR], FAR))
     ring_relay(wa.at[1], 1)
-    spread(wc.at[FAR, 1], 1, FAR)
+    ring_start(wc.at[FAR, 1], 1, FAR)
     shifted(has_near[0], rwhole, ("w",))
     wc[NEAR, 1] = (-couple(rwhole[...], NEAR)).reshape(4, 4, quarter // 4, m)
-    update_source(0)
+    shifted(has_near[0], rb.at[0, NEAR], ("b", 0, NEAR))
+    shifted(has_far[0], rb.at[0, FAR], ("b", 0, FAR))
+    source[...] = source[...] - couple(rb[0, NEAR], NEAR) - couple(rb[0, FAR], FAR)
 
     ring_end(wa.at[1], 1)
+    ring_relay(wc.at[FAR, 1], 1, FAR)
     invert(1)
     zq[1, NEAR] = solve(own(wc.at[NEAR, 1]))
     shift(has_near[1], zq.at[1, NEAR], rq.at[1, FAR, NEAR], ("q", 1, FAR, NEAR), near[1])
     zq[1, FAR] = solve(own(wc.at[FAR, 1]))
     shift(has_far[1], zq.at[1, FAR], rq.at[1, NEAR, FAR], ("q", 1, NEAR, FAR), far[1])
-    shift(has_near[1], zq.at[1, FAR], rq.at[1, FAR, FAR], ("q", 1, FAR, FAR), near[1])
-    shift(has_far[1], zq.at[1, NEAR], rq.at[1, NEAR, NEAR], ("q", 1, NEAR, NEAR), far[1])
     zb[1] = solve(source[...])
-    shift(has_near[1], zb.at[1], rb.at[1, FAR], ("b", 1, FAR), near[1])
-    shift(has_far[1], zb.at[1], rb.at[1, NEAR], ("b", 1, NEAR), far[1])
     hold(1, NEAR)
-    spread_end(wc.at[FAR, 1], 1, FAR)
+    ring_end(wc.at[FAR, 1], 1, FAR)
     hold(1, FAR)
     shifted(has_near[1], rq.at[1, NEAR, FAR], ("q", 1, NEAR, FAR))
     shifted(has_far[1], rq.at[1, FAR, NEAR], ("q", 1, FAR, NEAR))
+    shift(has_near[1], zq.at[1, FAR], rq.at[1, FAR, FAR], ("q", 1, FAR, FAR), near[1])
+    shift(has_far[1], zq.at[1, NEAR], rq.at[1, NEAR, NEAR], ("q", 1, NEAR, NEAR), far[1])
     put(wa.at[2], own(wa.at[1]) - couple(rq[1, NEAR, FAR], NEAR) - couple(rq[1, FAR, NEAR], FAR))
     ring_start(wa.at[2], 2)
+
+    def halves(h):
+        return pl.ds(half_rows * h, half_rows)
+
+    def send_half(h):
+        shift(has_near[1], zb.at[1, halves(h)], rb.at[1, FAR, halves(h)], ("b", 1, FAR, h), near[1])
+        shift(has_far[1], zb.at[1, halves(h)], rb.at[1, NEAR, halves(h)], ("b", 1, NEAR, h), far[1])
+
+    ring_relay(wa.at[2], 2)
+    send_half(0)
     shifted(has_near[1], rq.at[1, NEAR, NEAR], ("q", 1, NEAR, NEAR))
     put(wc.at[NEAR, 2], -couple(rq[1, NEAR, NEAR], NEAR))
+    ring_start(wc.at[NEAR, 2], 2, NEAR)
     shifted(has_far[1], rq.at[1, FAR, FAR], ("q", 1, FAR, FAR))
     put(wc.at[FAR, 2], -couple(rq[1, FAR, FAR], FAR))
-    ring_relay(wa.at[2], 2)
-    spread(wc.at[NEAR, 2], 2, NEAR)
-    spread(wc.at[FAR, 2], 2, FAR)
+    ring_start(wc.at[FAR, 2], 2, FAR)
+    send_half(1)
 
     ring_end(wa.at[2], 2)
     invert(2)
@@ -332,17 +311,21 @@
     shift(has_near[2], zq.at[2, NEAR, pl.ds(0, 32)], rq.at[2, FAR, NEAR, pl.ds(0, 32)], ("q", 2, FAR), near[2])
     zq[2, FAR, 0:32] = solve(wc[FAR, 2, z, y])
     shift(has_far[2], zq.at[2, FAR, pl.ds(0, 32)], rq.at[2, NEAR, FAR, pl.ds(0, 32)], ("q", 2, NEAR), far[2])
-    update_source(1)
+    ring_relay(wc.at[NEAR, 2], 2, NEAR)
+    ring_relay(wc.at[FAR, 2], 2, FAR)
     always = mirror >= 0
-    for c in range(4):
-        if c % 2 == 0:
-            here = pl.ds(chunk * c, half_rows)
-            zb[2, here] = solve(source[here])
-        here = pl.ds(chunk * c, chunk)
-        shift(always, zb.at[2, here], rb.at[2, 0, here], ("c", c), mirror)
-    spread_end(wc.at[NEAR, 2], 2, NEAR)
+    for h in range(2):
+        here = halves(h)
+        shifted(has_near[1], rb.at[1, NEAR, here], ("b", 1, NEAR, h))
+        shifted(has_far[1], rb.at[1, FAR, here], ("b", 1, FAR, h))
+        source[here] = source[here] - couple(rb[1, NEAR, here], NEAR) - couple(rb[1, FAR, here], FAR)
+        zb[2, here] = solve(source[here])
+        for c in (2 * h, 2 * h + 1):
+            there = pl.ds(chunk * c, chunk)
+            shift(always, zb.at[2, there], rb.at[2, 0, there], ("c", c), mirror)
+    ring_end(wc.at[NEAR, 2], 2, NEAR)
     hold(2, NEAR)
-    spread_end(wc.at[FAR, 2], 2, FAR)
+    ring_end(wc.at[FAR, 2], 2, FAR)
     hold(2, FAR)
     shifted(has_near[2], rq.at[2, NEAR, FAR, pl.ds(0, 32)], ("q", 2, NEAR))
     shifted(has_far[2], rq.at[2, FAR, NEAR, pl.ds(0, 32)], ("q", 2, FAR))
@@ -353,12 +336,12 @@
         arrived(rb.at[2, 0, here], ("c", c))
         shift(has_onward, rb.at[2, 0, here], rb.at[2, 1, here], ("d", c), onward)
         if c % 2 == 1:
-            here = pl.ds(chunk * (c - 1), half_rows)
+            here = halves(c // 2)
             source[here] = source[here] - couple(rb[2, 0, here], direct)
     for c in range(4):
         shifted(has_backward, rb.at[2, 1, pl.ds(chunk * c, chunk)], ("d", c))
         if c % 2 == 1:
-            here = pl.ds(chunk * (c - 1), half_rows)
+            here = halves(c // 2)
             source[here] = source[here] - couple(rb[2, 1, here], 1 - direct)
     b_out[...] = source[...].T
 

time: 136 us -> 125 us (0.919)
  Pallas kernels: 131 us -> 119 us
    pallas_call x1, Pallas kernels: 131 us -> 119 us  [shards(): pl.pallas_call(functools.partial(kernel, sectors, m), out_shape=(jax.Shap...]
where the time goes in v3:
time: 125 us; the launch traced here: 123 us
  Pallas kernels  119 us (95%)
  local copies, waits for them, and re-layouts  3.34 us (3%)
    pallas_call x1, Pallas kernels, shards(): pl.pallas_call(functools.partial(kernel, sectors, m), out_shape=(jax.Shap...  119 us
    unnamed x2, local copies, waits for them, and re-layouts  3.34 us

profile of v3, /device:TPU:6, one launch (start us, length us, event | category | flops | bytes accessed | tf_op | source)
XLA Modules:
  0.0 123.1 jit_solution(14334728827570788084)
XLA Ops:
  0.6 119.2 %reduction.1 = (f32[32,512]{1,0:T(8,128)}, f32[512,256]{1,0:T(8,128)}) custom-call(f32[32,512]{1,0:T(8,128)} %bitcast.17, f32[32,512]{1,0:T(8,128)} %bitcast.18, f32[32,512]{1,0:T(8,128)} %bitcast.19, f32[512,256]{1,0:T(8,128)} %bitcast.14), custom_call_target="tpu_custom_call" | custom-call | tf_op jit(solution)/shard_map/reduction/pallas_call | solution.py:363
  119.8 1.5 %copy.8 = f32[1,512,32]{1,2,0:T(8,128)} copy(f32[1,512,32]{1,2,0:T(8,128)} %bitcast.16) | data formatting | bytes 131072
  121.3 1.9 %copy.9 = f32[1,512,256]{2,1,0:T(8,128)} copy(f32[1,512,256]{2,1,0:T(8,128)} %bitcast.15) | data formatting | bytes 1048576

commit v4 on v3

--- a/solution.py
+++ b/solution.py
@@ -47,7 +47,6 @@
     side = 1 - 2 * ((sec % 8) // 4)
     quarter = m // 4
     half_rows = source.shape[0] // 2
-    chunk = source.shape[0] // 4
 
     loads = [
         pltpu.make_async_copy(a_in, wa.at[0, z, y], load_sem.at[0]),
@@ -139,7 +138,18 @@
     def y_send(i, r):
         push(slab(i, r, 0), ("y", i, r, 1), y_next)
         push(slab(i, r, 0), ("y", i, r, 3), y_prev)
-        push(slab(i, r, 0), ("y", i, r, 2), y_far)
+        if r % 2 == 0:
+            push(slab(i, r, 0), ("y", i, r, 2), y_far)
+
+    def y_half(i, r, dy, part):
+        return whole[i].at[zat(r), yat(dy), pl.ds(16 * part, 16)]
+
+    def y_relay(i):
+        for r in (3, 1):
+            arrived(slab(i, r, 3), ("y", i, r, 1))
+            push(y_half(i, r, 3, 0), ("yy", i, r, 1), y_next)
+            arrived(slab(i, r, 1), ("y", i, r, 3))
+            push(y_half(i, r, 1, 1), ("yy", i, r, 3), y_prev)
 
     def z_relay(i):
         arrived(slab(i, 3, 0), ("z", i, 1))
@@ -154,11 +164,21 @@
         arrived(half(i, 2, 1), ("zz", i, 3))
         y_send(i, 2)
 
-    def y_last(i):
-        for r in range(4):
+    seen = set()
+
+    def y_wait(i, r):
+        if (i, r) not in seen:
+            seen.add((i, r))
             arrived(slab(i, r, 3), ("y", i, r, 1))
             arrived(slab(i, r, 1), ("y", i, r, 3))
+
+    def y_last(i):
+        for r in (0, 2):
+            y_wait(i, r)
             arrived(slab(i, r, 2), ("y", i, r, 2))
+        for r in (1, 3):
+            arrived(y_half(i, r, 2, 0), ("yy", i, r, 1))
+            arrived(y_half(i, r, 2, 1), ("yy", i, r, 3))
 
     def part(ref, dy, p):
         return ref.at[pl.ds(2 * p, 2), yat(dy)]
@@ -212,7 +232,6 @@
         c_hi[role], c_lo[role] = split(rows(wc.at[role, k]))
 
     z_own(0)
-    z_own(1)
     y_send(0, 0)
     y_send(1, 0)
     y_send(2, 0)
@@ -231,16 +250,21 @@
     clear(has_near[1], rb.at[1, NEAR])
     clear(has_far[1], rb.at[1, FAR])
     clear(has_backward, rb.at[2, 1])
+    y_wait(0, 0)
+    z_own(1)
     z_relay(0)
     z_own(2)
+    y_relay(0)
     z_relay(1)
+    y_relay(1)
     z_last(0)
     z_relay(2)
-    z_last(1)
-    z_last(2)
-
     y_last(0)
     invert(0)
+    z_last(1)
+    y_relay(2)
+    z_last(2)
+
     zq[0, FAR] = solve(own(wc.at[FAR, 0]))
     shift(has_far[0], zq.at[0, FAR], rq.at[0, FAR, FAR], ("q", 0, FAR, FAR), far[0])
     zq[0, NEAR] = solve(own(wc.at[NEAR, 0]))
@@ -270,6 +294,13 @@
     shifted(has_far[0], rb.at[0, FAR], ("b", 0, FAR))
     source[...] = source[...] - couple(rb[0, NEAR], NEAR) - couple(rb[0, FAR], FAR)
 
+    def halves(h):
+        return pl.ds(half_rows * h, half_rows)
+
+    def send_half(h):
+        shift(has_near[1], zb.at[1, halves(h)], rb.at[1, FAR, halves(h)], ("b", 1, FAR, h), near[1])
+        shift(has_far[1], zb.at[1, halves(h)], rb.at[1, NEAR, halves(h)], ("b", 1, NEAR, h), far[1])
+
     ring_end(wa.at[1], 1)
     ring_relay(wc.at[FAR, 1], 1, FAR)
     invert(1)
@@ -287,14 +318,6 @@
     shift(has_far[1], zq.at[1, NEAR], rq.at[1, NEAR, NEAR], ("q", 1, NEAR, NEAR), far[1])
     put(wa.at[2], own(wa.at[1]) - couple(rq[1, NEAR, FAR], NEAR) - couple(rq[1, FAR, NEAR], FAR))
     ring_start(wa.at[2], 2)
-
-    def halves(h):
-        return pl.ds(half_rows * h, half_rows)
-
-    def send_half(h):
-        shift(has_near[1], zb.at[1, halves(h)], rb.at[1, FAR, halves(h)], ("b", 1, FAR, h), near[1])
-        shift(has_far[1], zb.at[1, halves(h)], rb.at[1, NEAR, halves(h)], ("b", 1, NEAR, h), far[1])
-
     ring_relay(wa.at[2], 2)
     send_half(0)
     shifted(has_near[1], rq.at[1, NEAR, NEAR], ("q", 1, NEAR, NEAR))
@@ -314,15 +337,30 @@
     ring_relay(wc.at[NEAR, 2], 2, NEAR)
     ring_relay(wc.at[FAR, 2], 2, FAR)
     always = mirror >= 0
-    for h in range(2):
-        here = halves(h)
-        shifted(has_near[1], rb.at[1, NEAR, here], ("b", 1, NEAR, h))
-        shifted(has_far[1], rb.at[1, FAR, here], ("b", 1, FAR, h))
-        source[here] = source[here] - couple(rb[1, NEAR, here], NEAR) - couple(rb[1, FAR, here], FAR)
-        zb[2, here] = solve(source[here])
-        for c in (2 * h, 2 * h + 1):
-            there = pl.ds(chunk * c, chunk)
-            shift(always, zb.at[2, there], rb.at[2, 0, there], ("c", c), mirror)
+    pieces = 8
+    ahead = 4
+    step = source.shape[0] // pieces
+
+    def piece(c):
+        return pl.ds(step * c, step)
+
+    def send_piece(c):
+        if c % (pieces // 2) == 0:
+            h = c // (pieces // 2)
+            here = halves(h)
+            shifted(has_near[1], rb.at[1, NEAR, here], ("b", 1, NEAR, h))
+            shifted(has_far[1], rb.at[1, FAR, here], ("b", 1, FAR, h))
+            source[here] = source[here] - couple(rb[1, NEAR, here], NEAR) - couple(rb[1, FAR, here], FAR)
+            zb[2, here] = solve(source[here])
+        shift(always, zb.at[2, piece(c)], rb.at[2, 0, piece(c)], ("c", c), mirror)
+
+    for c in range(ahead):
+        send_piece(c)
+    for c in range(pieces):
+        arrived(rb.at[2, 0, piece(c)], ("c", c))
+        shift(has_onward, rb.at[2, 0, piece(c)], rb.at[2, 1, piece(c)], ("d", c), onward)
+        if c + ahead < pieces:
+            send_piece(c + ahead)
     ring_end(wc.at[NEAR, 2], 2, NEAR)
     hold(2, NEAR)
     ring_end(wc.at[FAR, 2], 2, FAR)
@@ -331,17 +369,11 @@
     shifted(has_far[2], rq.at[2, FAR, NEAR, pl.ds(0, 32)], ("q", 2, FAR))
     a_out[...] = wa[2, z, y] - couple(rq[2, NEAR, FAR, 0:32], NEAR) - couple(rq[2, FAR, NEAR, 0:32], FAR)
     direct = (1 - toward * side) // 2
-    for c in range(4):
-        here = pl.ds(chunk * c, chunk)
-        arrived(rb.at[2, 0, here], ("c", c))
-        shift(has_onward, rb.at[2, 0, here], rb.at[2, 1, here], ("d", c), onward)
-        if c % 2 == 1:
-            here = halves(c // 2)
-            source[here] = source[here] - couple(rb[2, 0, here], direct)
-    for c in range(4):
-        shifted(has_backward, rb.at[2, 1, pl.ds(chunk * c, chunk)], ("d", c))
-        if c % 2 == 1:
-            here = halves(c // 2)
+    source[...] = source[...] - couple(rb[2, 0], direct)
+    for c in range(pieces):
+        shifted(has_backward, rb.at[2, 1, piece(c)], ("d", c))
+        if (c + 1) % (pieces // 2) == 0:
+            here = halves(c // (pieces // 2))
             source[here] = source[here] - couple(rb[2, 1, here], 1 - direct)
     b_out[...] = source[...].T
 

time: 125 us -> 123 us (0.984)
  no operation moved by 1% of the time
where the time goes in v4:
time: 123 us; the launch traced here: 122 us
  Pallas kernels  118 us (96%)
  local copies, waits for them, and re-layouts  3.34 us (3%)
    pallas_call x1, Pallas kernels, shards(): pl.pallas_call(functools.partial(kernel, sectors, m), out_shape=(jax.Shap...  118 us
    unnamed x2, local copies, waits for them, and re-layouts  3.34 us

profile of v4, /device:TPU:6, one launch (start us, length us, event | category | flops | bytes accessed | tf_op | source)
XLA Modules:
  0.0 122.1 jit_solution(14165477420785858587)
XLA Ops:
  0.6 118.1 %reduction.1 = (f32[32,512]{1,0:T(8,128)}, f32[512,256]{1,0:T(8,128)}) custom-call(f32[32,512]{1,0:T(8,128)} %bitcast.17, f32[32,512]{1,0:T(8,128)} %bitcast.18, f32[32,512]{1,0:T(8,128)} %bitcast.19, f32[512,256]{1,0:T(8,128)} %bitcast.14), custom_call_target="tpu_custom_call" | custom-call | tf_op jit(solution)/shard_map/reduction/pallas_call | solution.py:395
  118.7 1.5 %copy.8 = f32[1,512,32]{1,2,0:T(8,128)} copy(f32[1,512,32]{1,2,0:T(8,128)} %bitcast.16) | data formatting | bytes 131072
  120.2 1.9 %copy.9 = f32[1,512,256]{2,1,0:T(8,128)} copy(f32[1,512,256]{2,1,0:T(8,128)} %bitcast.15) | data formatting | bytes 1048576

commit v5 on v4

--- a/solution.py
+++ b/solution.py
@@ -25,7 +25,9 @@
 
 def product(left, hi, lo):
     left_hi, left_lo = split(left)
-    return dot(left_hi, hi) + (dot(left_lo, hi) + dot(left_hi, lo))
+    count = left.shape[0]
+    both = dot(jnp.concatenate([left_hi, left_lo], axis=0), hi)
+    return both[:count] + (both[count:] + dot(left_hi, lo))
 
 
 class Slots:

time: 123 us -> 122 us (level)
  no operation moved by 1% of the time
where the time goes in v5:
time: 122 us
  Pallas kernels  118 us (97%)
  local copies, waits for them, and re-layouts  3.34 us (3%)
    pallas_call x1, Pallas kernels, shards(): pl.pallas_call(functools.partial(kernel, sectors, m), out_shape=(jax.Shap...  118 us
    unnamed x2, local copies, waits for them, and re-layouts  3.34 us

profile of v5, /device:TPU:6, one launch (start us, length us, event | category | flops | bytes accessed | tf_op | source)
XLA Modules:
  0.0 121.9 jit_solution(6803802789269603306)
XLA Ops:
  0.6 117.9 %reduction.1 = (f32[32,512]{1,0:T(8,128)}, f32[512,256]{1,0:T(8,128)}) custom-call(f32[32,512]{1,0:T(8,128)} %bitcast.17, f32[32,512]{1,0:T(8,128)} %bitcast.18, f32[32,512]{1,0:T(8,128)} %bitcast.19, f32[512,256]{1,0:T(8,128)} %bitcast.14), custom_call_target="tpu_custom_call" | custom-call | tf_op jit(solution)/shard_map/reduction/pallas_call | solution.py:397
  118.6 1.5 %copy.8 = f32[1,512,32]{1,2,0:T(8,128)} copy(f32[1,512,32]{1,2,0:T(8,128)} %bitcast.16) | data formatting | bytes 131072
  120.0 1.9 %copy.9 = f32[1,512,256]{2,1,0:T(8,128)} copy(f32[1,512,256]{2,1,0:T(8,128)} %bitcast.15) | data formatting | bytes 1048576
